TPU v7x, 32 devices: a whole 2x2x4 slice. The times are simulated.
32 devices in a mesh: mem: 4 (over z), sp: 8 (over y, x, core).
Axes of the slice: x: 2, y: 2, z: 4, core: 2. Of those that a mesh axis runs over, the one named last changes fastest.
Arguments:
- span_input: bfloat16 [4, 1024, 5120], P('mem', 'sp'), may hold values from -6 to 6
- w_query: bfloat16 [5120, 4096], P(None, 'sp')
- w_key: bfloat16 [5120, 4096], P(None, 'sp')
- w_value: bfloat16 [5120, 4096], P(None, 'sp'), may hold values from -0.078125 to 0.078125
- memory_kv: bfloat16 [32, 2, 256, 4096], P(('mem', 'sp')), may hold values from -6 to 6
- selected: int32 [4, 8], replicated, may hold values from 0 to 31, as said below
- frame_slot: int32 [32], replicated, may hold values from 0 to 31, as said below
- write_slot: int32 [4, 2], replicated, may hold values from 0 to 31, as said below
Outputs:
- attended: bfloat16 [4, 1024, 4096], P('mem', None, 'sp')
- new_memory: bfloat16 [32, 2, 256, 4096], P(('mem', 'sp'))
Inputs may be any that keep to these rules, and one draw needn't show every extreme that they name: `selected`: each row names 8 different frame ids. Of one row's frames, at most 2 have their slot in one block of 8 consecutive slots, and in every row some block holds exactly 2 of them. `frame_slot`: every slot appears exactly once. `write_slot`: all entries differ; the 2 slots of one row lie in different blocks of 8 consecutive slots, and every such block holds exactly 2 entries.
All inputs are finite; a program needn't handle non-finite values.
Results may differ from a plain program's by a relative error of at most 0.0085.
Values may be sent and summed in bfloat16 or wider, within the bound.
A program may use at most 128 MiB of HBM per device.

v0:
```python
import functools
import math

import jax
import jax.numpy as jnp
from jax import lax
from jax.experimental import pallas as pl
from jax.experimental.pallas import tpu as pltpu
from jax.sharding import PartitionSpec as P

HD = 128
MTOK = 256
FRAMES_SPAN = 2
CAP = 2
SEL = 8
HALVES = 2
CHUNKS = 2 * HALVES
TOK = MTOK // HALVES
NEG_FILL = -1e30
MESH = pl.DeviceIdType.MESH
VMEM_LIMIT = 58 * 1024 * 1024


def greet(groups, width, g, c):
    barrier = pltpu.get_barrier_semaphore()
    for o in range(1, width):
        pl.semaphore_signal(
            barrier, inc=1, device_id=(g, lax.rem(c + o, width)), device_id_type=MESH
        )
    for o in range(1, groups):
        pl.semaphore_signal(
            barrier, inc=1, device_id=(lax.rem(g + o, groups), c), device_id_type=MESH
        )
    pl.semaphore_wait(barrier, width + groups - 2)


def project_kernel(groups, width, pool, pick, x, wq, wk, wv, mem, qkv, pooled, got, *scratch):
    rows = scratch[:CHUNKS]
    (sendbuf, xg, w3, w_sem, own_sem, mem_send, mem_recv, x_send, x_recv, f_send, f_recv,
     z_send, z_recv, z_own) = scratch[CHUNKS:]
    g = lax.axis_index("mem")
    c = lax.axis_index("sp")
    cols = wq.shape[1]
    block = x.shape[0]
    pairs = width // 2
    me_pair = c // 2
    lane = lax.rem(c, 2)
    sibling = me_pair * 2 + 1 - lane
    lane_rows = pl.ds(pl.multiple_of(lane * block, block), block)
    greet(groups, width, g, c)

    own = []
    sends = []

    def mem_copy(ch, o):
        to = lax.rem(c + o, width)
        return pltpu.make_async_remote_copy(
            src_ref=mem.at[pl.ds(ch * TOK, TOK), pl.ds(pl.multiple_of(to * cols, cols), cols)],
            dst_ref=rows[ch].at[c],
            send_sem=mem_send.at[ch, o],
            recv_sem=mem_recv.at[ch, o],
            device_id=(g, to),
            device_id_type=MESH,
        )

    def x_copy(j):
        to = sibling if j == 0 else lax.rem(c + 2 * j, width)
        return pltpu.make_async_remote_copy(
            src_ref=x,
            dst_ref=xg.at[me_pair, lane_rows],
            send_sem=x_send.at[j],
            recv_sem=x_recv.at[j],
            device_id=(g, to),
            device_id_type=MESH,
        )

    def send_mem(ch):
        copy = pltpu.make_async_copy(
            mem.at[pl.ds(ch * TOK, TOK), pl.ds(pl.multiple_of(c * cols, cols), cols)],
            rows[ch].at[c],
            own_sem.at[ch],
        )
        copy.start()
        own.append(copy)
        for o in range(1, width):
            copy = mem_copy(ch, o)
            copy.start()
            sends.append(copy)

    def send_x(j):
        copy = x_copy(j)
        copy.start()
        sends.append(copy)

    own_x = pltpu.make_async_copy(x, xg.at[me_pair, lane_rows], own_sem.at[CHUNKS])
    w_copies = [
        pltpu.make_async_copy(w, w3.at[i], w_sem.at[i]) for i, w in enumerate((wq, wk, wv))
    ]
    send_mem(0)
    send_x(0)
    own_x.start()
    for copy in w_copies:
        copy.start()
    for step in range(1, max(CHUNKS, pairs)):
        if step < CHUNKS:
            send_mem(step)
        if step < pairs:
            send_x(step)

    z_copies = []
    z_local = []

    def fetch(ch):
        own[ch].wait()
        for o in range(1, width):
            mem_copy(ch, o).wait_recv()
        for o in list(range(1, groups)) + [0]:
            to = lax.rem(g + o, groups)
            for r in range(CAP):
                sendbuf[ch, to, r] = rows[ch][pick[to * CAP + r]]
            if o == 0:
                copy = pltpu.make_async_copy(sendbuf.at[ch, g], got.at[ch, g], z_own.at[ch])
                z_local.append(copy)
            else:
                copy = pltpu.make_async_remote_copy(
                    src_ref=sendbuf.at[ch, to],
                    dst_ref=got.at[ch, g],
                    send_sem=z_send.at[ch, o],
                    recv_sem=z_recv.at[ch, o],
                    device_id=(to, c),
                    device_id_type=MESH,
                )
                z_copies.append(copy)
            copy.start()

    small = 2 * block // pool
    row_id = lax.broadcasted_iota(jnp.int32, (small, 2 * block), 0) * pool
    col_id = lax.broadcasted_iota(jnp.int32, (small, 2 * block), 1)
    inside = (col_id >= row_id) & (col_id < row_id + pool)
    averager = jnp.where(inside, 1.0 / pool, 0.0).astype(jnp.bfloat16)
    forwards = []

    def project(j):
        pair = lax.rem(me_pair - j + pairs, pairs)
        x_copy(j).wait_recv()
        if j == 0:
            own_x.wait()
            for copy in w_copies:
                copy.wait()
        else:
            copy = pltpu.make_async_remote_copy(
                src_ref=xg.at[pair, lane_rows],
                dst_ref=xg.at[pair, lane_rows],
                send_sem=f_send.at[j],
                recv_sem=f_recv.at[j],
                device_id=(g, sibling),
                device_id_type=MESH,
            )
            copy.start()
            forwards.append(copy)
            copy.wait_recv()
        out_rows = pl.ds(pl.multiple_of(pair * 2 * block, 2 * block), 2 * block)

        def one(i, carry):
            part = jnp.dot(xg[pair], w3[i], preferred_element_type=jnp.float32)
            qkv[i, out_rows, :] = part.astype(jnp.bfloat16)
            return carry

        lax.fori_loop(0, 3, one, 0)
        small_rows = pl.ds(pl.multiple_of(pair * small, small), small)
        for i in range(2):
            mean = jnp.dot(averager, qkv[i + 1, out_rows, :], preferred_element_type=jnp.float32)
            pooled[i, small_rows, :] = mean.astype(jnp.bfloat16)

    for step in range(max(CHUNKS, pairs)):
        if step < CHUNKS:
            fetch(step)
        if step < pairs:
            project(step)

    for copy in sends + forwards:
        copy.wait_send()
    for copy in z_local:
        copy.wait()
    for copy in z_copies:
        copy.wait()


def attend_kernel(groups, width, wsel, rsel, bias, qkv, got, pooled, att, assembled, *scratch):
    arrived = scratch[:CHUNKS]
    wbuf, rbuf, z_send, z_recv, r_send, r_recv, r_own = scratch[CHUNKS:]
    g = lax.axis_index("mem")
    c = lax.axis_index("sp")
    span, cols = att.shape
    heads = cols // HD
    half = got.shape[0] // 2
    greet(groups, width, g, c)
    z_copies = []
    for ch in range(CHUNKS):
        for o in list(range(1, groups)) + [0]:
            to = lax.rem(g + o, groups)
            piece = pooled[ch // HALVES, wsel[to], ch % HALVES]
            if o == 0:
                arrived[ch][g] = piece
                continue
            wbuf[ch, to] = piece
            copy = pltpu.make_async_remote_copy(
                src_ref=wbuf.at[ch, to],
                dst_ref=arrived[ch].at[g],
                send_sem=z_send.at[ch, o],
                recv_sem=z_recv.at[ch, o],
                device_id=(to, c),
                device_id_type=MESH,
            )
            copy.start()
            z_copies.append((ch, copy))

    r_copies = []
    r_local = []

    def regroup(ch):
        for at, copy in z_copies:
            if at == ch:
                copy.wait_recv()
        for o in list(range(1, width)) + [0]:
            to = lax.rem(c + o, width)
            rbuf[ch, to] = arrived[ch][rsel[to]]
            place = assembled.at[
                pl.ds(ch * TOK, TOK), pl.ds(pl.multiple_of(c * cols, cols), cols)
            ]
            if o == 0:
                copy = pltpu.make_async_copy(rbuf.at[ch, to], place, r_own.at[ch])
                r_local.append(copy)
            else:
                copy = pltpu.make_async_remote_copy(
                    src_ref=rbuf.at[ch, to],
                    dst_ref=place,
                    send_sem=r_send.at[ch, o],
                    recv_sem=r_recv.at[ch, o],
                    device_id=(g, to),
                    device_id_type=MESH,
                )
                r_copies.append(copy)
            copy.start()

    factor = HD ** (-0.5) * math.log2(math.e)
    block = min(256, span)
    nt = (((1,), (1,)), ((), ()))

    def attend(h):
        lanes = slice(h * HD, (h + 1) * HD)

        def one(i, carry):
            rows = pl.ds(pl.multiple_of(i * block, block), block)
            query = qkv[0, rows, lanes]
            own = lax.dot_general(query, qkv[1, :, lanes], nt, preferred_element_type=jnp.float32)
            far = lax.dot_general(
                query, got[0:half, lanes], nt, preferred_element_type=jnp.float32
            )
            if bias is not None:
                far = far + bias[...]
            peak = jnp.maximum(
                jnp.max(own, axis=1, keepdims=True), jnp.max(far, axis=1, keepdims=True)
            )
            own = jnp.exp2((own - peak) * factor)
            far = jnp.exp2((far - peak) * factor)
            totals = jnp.sum(own, axis=1, keepdims=True) + jnp.sum(far, axis=1, keepdims=True)
            mixed = jnp.dot(
                own.astype(jnp.bfloat16), qkv[2, :, lanes], preferred_element_type=jnp.float32
            )
            mixed += jnp.dot(
                far.astype(jnp.bfloat16),
                got[half : 2 * half, lanes],
                preferred_element_type=jnp.float32,
            )
            att[rows, lanes] = (mixed / totals).astype(jnp.bfloat16)
            return carry

        lax.fori_loop(0, span // block, one, 0)

    for step in range(max(heads, CHUNKS)):
        if step < heads:
            attend(step)
        if step < CHUNKS:
            regroup(step)
    for _, copy in z_copies:
        copy.wait_send()
    for copy in r_local:
        copy.wait()
    for copy in r_copies:
        copy.wait()


def local(span_input, w_query, w_key, w_value, memory_kv, selected, frame_slot, write_slot):
    groups = lax.axis_size("mem")
    width = lax.axis_size("sp")
    g = lax.axis_index("mem")
    c = lax.axis_index("sp")
    depth, cols = w_query.shape
    block = span_input.shape[1]
    span = block * width
    pairs = width // 2
    pool = span // (FRAMES_SPAN * MTOK)
    features = memory_kv.shape[3]

    slot_ids = jnp.take(frame_slot, selected, axis=0)
    slot_row = slot_ids // width
    in_row = slot_row == g
    rank = jnp.cumsum(in_row.astype(jnp.int32), axis=1) - 1
    hit = in_row[:, None, :] & (rank[:, None, :] == jnp.arange(CAP, dtype=jnp.int32)[None, :, None])
    pick = jnp.sum(jnp.where(hit, (slot_ids % width)[:, None, :], 0), axis=2).reshape(-1)

    vmem = pl.BlockSpec(memory_space=pltpu.VMEM)
    smem = pl.BlockSpec(memory_space=pltpu.SMEM)
    anywhere = pl.BlockSpec(memory_space=pl.ANY)
    bf16 = jnp.bfloat16
    dma = pltpu.SemaphoreType.DMA
    qkv, pooled, got = pl.pallas_call(
        functools.partial(project_kernel, groups, width, pool),
        out_shape=(
            jax.ShapeDtypeStruct((3, span, cols), bf16),
            jax.ShapeDtypeStruct((2, FRAMES_SPAN * MTOK, cols), bf16),
            jax.ShapeDtypeStruct((CHUNKS, groups, CAP, TOK, cols), bf16),
        ),
        in_specs=[smem] + [anywhere] * 5,
        out_specs=(vmem, vmem, anywhere),
        scratch_shapes=[pltpu.VMEM((width, TOK, cols), bf16)] * CHUNKS
        + [
            pltpu.VMEM((CHUNKS, groups, CAP, TOK, cols), bf16),
            pltpu.VMEM((pairs, 2 * block, depth), bf16),
            pltpu.VMEM((3, depth, cols), bf16),
            dma((3,)),
            dma((CHUNKS + 1,)),
            dma((CHUNKS, width)),
            dma((CHUNKS, width)),
            dma((pairs,)),
            dma((pairs,)),
            dma((pairs,)),
            dma((pairs,)),
            dma((CHUNKS, groups)),
            dma((CHUNKS, groups)),
            dma((CHUNKS,)),
        ],
        compiler_params=pltpu.CompilerParams(
            collective_id=0, has_side_effects=True, vmem_limit_bytes=VMEM_LIMIT
        ),
        name="project_and_fetch",
    )(pick, span_input[0], w_query, w_key, w_value, memory_kv.reshape(2 * MTOK, features))

    own_slots = lax.dynamic_index_in_dim(write_slot, g, 0, keepdims=False)
    rows_m = jnp.arange(groups, dtype=jnp.int32)
    frames = jnp.arange(FRAMES_SPAN, dtype=jnp.int32)
    wsel = jnp.sum(
        jnp.where((own_slots // width)[None, :] == rows_m[:, None], frames[None, :], 0), axis=1
    )
    targets = g * width + jnp.arange(width, dtype=jnp.int32)
    match = jnp.any(write_slot[None, :, :] == targets[:, None, None], axis=2)
    rsel = jnp.sum(jnp.where(match, rows_m[None, :], 0), axis=1)

    operands = [wsel, rsel]
    specs = [smem, smem]
    kernel = functools.partial(attend_kernel, groups, width)
    if groups * CAP != SEL:
        own_rows = lax.dynamic_index_in_dim(slot_row, g, 0, keepdims=False)
        counts = jnp.sum((own_rows[None, :] == rows_m[:, None]).astype(jnp.int32), axis=1)
        live = jnp.arange(CAP, dtype=jnp.int32)[None, :] < counts[:, None]
        fill = jnp.where(live, 0.0, NEG_FILL).astype(jnp.float32)
        fill = jnp.broadcast_to(fill[None, :, :, None], (HALVES, groups, CAP, TOK))
        operands.append(fill.reshape(1, -1))
        specs.append(vmem)
    else:
        kernel = functools.partial(without_bias, kernel)
    attended, assembled = pl.pallas_call(
        kernel,
        out_shape=(
            jax.ShapeDtypeStruct((span, cols), bf16),
            jax.ShapeDtypeStruct((2 * MTOK, features), bf16),
        ),
        in_specs=specs + [vmem] * 3,
        out_specs=(vmem, anywhere),
        scratch_shapes=[pltpu.VMEM((groups, TOK, cols), bf16)] * CHUNKS
        + [
            pltpu.VMEM((CHUNKS, groups, TOK, cols), bf16),
            pltpu.VMEM((CHUNKS, width, TOK, cols), bf16),
            dma((CHUNKS, groups)),
            dma((CHUNKS, groups)),
            dma((CHUNKS, width)),
            dma((CHUNKS, width)),
            dma((CHUNKS,)),
        ],
        compiler_params=pltpu.CompilerParams(
            collective_id=1, has_side_effects=True, vmem_limit_bytes=VMEM_LIMIT
        ),
        name="attend_and_write",
    )(
        *operands,
        qkv,
        got.reshape(-1, cols),
        pooled.reshape(2, FRAMES_SPAN, HALVES, TOK, cols),
    )
    written = jnp.any(write_slot == g * width + c)
    new_memory = jnp.where(written, assembled.reshape(memory_kv.shape), memory_kv)
    return (attended[None], new_memory)


def without_bias(kernel, wsel, rsel, *rest):
    kernel(wsel, rsel, None, *rest)


def solution(mesh):
    placed = (
        P("mem", "sp", None),
        P(None, "sp"),
        P(None, "sp"),
        P(None, "sp"),
        P(("mem", "sp"), None, None, None),
        P(),
        P(),
        P(),
    )
    return jax.shard_map(
        local,
        mesh=mesh,
        in_specs=placed,
        out_specs=(P("mem", None, "sp"), P(("mem", "sp"), None, None, None)),
        check_vma=False,
    )
```

profile of v0, /device:TPU:11, one launch (start us, length us, event | category | flops | bytes accessed | tf_op | source)
XLA Modules:
  0.0 226.7 jit_solution(11112311839991130165)
XLA Ops:
  0.6 0.0 copy-start
  0.7 1.3 compare_reduce_fusion.1
  2.0 0.9 fusion.4
  2.8 0.6 fusion.3.wsel
  3.4 0.8 compare_reduce_fusion
  4.2 0.5 select_reduce_fusion.1.rsel
  4.7 0.7 compare_select_fusion
  5.4 0.1 reshape.79
  5.5 0.0 copy-done
  5.5 0.7 gather_fusion
  6.2 0.1 reshape.78
  6.3 0.7 fusion.5
  7.0 0.2 reduce_window_sum.11
  7.2 0.7 add_select_fusion
  7.9 0.1 select_reduce_fusion
  8.0 0.1 copy.12
  8.1 0.6 reshape.72.pick
  8.8 117.9 %project_and_fetch.1 = (bf16[3,1024,512]{2,1,0:T(8,128)(2,1)}, bf16[2,512,512]{2,1,0:T(8,128)(2,1)}, bf16[4,4,2,128,512]{4,3,2,1,0:T(8,128)(2,1)}) custom-call(s32[8]{0:T(128)} %reshape.72.pick, bf16[128,5120]{1,0:T(8,128)(2,1)} %bitcast.9, bf16[5120,512]{1,0:T(8,128)(2,1)} %wq.1, bf16[5120,512]{1,0:T(8,128)(2,1)} %wk.1, bf16[5120,512]{1,0:T(8,128)(2,1)} %wv.1, ...), custom_call_target="tpu_custom_call" | custom-call | tf_op jit(solution)/shard_map/project_and_fetch/pallas_call | solution.py:318
  126.6 0.0 copy-start.1
  126.6 95.7 %attend_and_write.1 = (bf16[1024,512]{1,0:T(8,128)(2,1)}, bf16[512,4096]{1,0:T(8,128)(2,1)}) custom-call(s32[4]{0:T(128)} %fusion.3.wsel, s32[8]{0:T(128)} %select_reduce_fusion.1.rsel, bf16[3,1024,512]{2,1,0:T(8,128)(2,1)} %get-tuple-element.7.rest_0_, bf16[4096,512]{1,0:T(8,128)(2,1)} %bitcast.7, bf16[2,2,2,128,512]{4,3,2,1,0:T(8,128)(2,1)} %bitcast.10), custom_call_target="tpu_custom_call" | custom-call | tf_op jit(solution)/shard_map/attend_and_write/pallas_call | solution.py:373
  222.4 0.0 copy-done.1
  222.4 3.4 %broadcast_select_fusion = bf16[1,2,256,4096]{3,2,1,0:T(8,128)(2,1)} fusion(bf16[1,2,256,4096]{3,2,1,0:T(8,128)(2,1)} %bitcast.8, bf16[1,2,256,4096]{3,2,1,0:T(8,128)(2,1)S(1)} %copy-done.1, pred[]{:T(512)} %compare_reduce_fusion.1), kind=kLoop, calls=%fused_computation.1 | loop fusion | flops 2097152 | bytes 12582913 | tf_op jit(solution)/shard_map/jit(_where)/select_n | solution.py:402
  225.8 0.0 copy-done.2
  225.8 1.0 copy.14
  (3 shorter events, 0.0 us)
Async XLA Ops:
  0.6 4.9 %copy-start = (s32[32]{0:T(128)S(1)}, s32[32]{0:T(128)}, u32[]{:S(2)}) copy-start(s32[32]{0:T(128)} %param.14) | copy-start | bytes 388
  126.6 95.8 %copy-start.1 = (bf16[1,2,256,4096]{3,2,1,0:T(8,128)(2,1)S(1)}, bf16[1,2,256,4096]{3,2,1,0:T(8,128)(2,1)}, u32[]{:S(2)}) copy-start(bf16[1,2,256,4096]{3,2,1,0:T(8,128)(2,1)} %param.12) | copy-start | bytes 12582916
  222.4 3.4 %copy-start.2 = (bf16[1024,512]{1,0:T(8,128)(2,1)S(1)}, bf16[1024,512]{1,0:T(8,128)(2,1)}, u32[]{:S(2)}) copy-start(bf16[1024,512]{1,0:T(8,128)(2,1)} %get-tuple-element.10) | copy-start | bytes 3145732
where the time goes:
time: 228 us; the launch traced here: 227 us
  Pallas kernels  214 us (94%)
  other arithmetic  9.86 us (4%)
  local copies, waits for them, and re-layouts  2.59 us (1%)
    pallas_call x1, Pallas kernels, local(): pl.pallas_call(functools.partial(project_kernel, groups, width, pool), ou...  118 us
    pallas_call x1, Pallas kernels, local(): pl.pallas_call(kernel, out_shape=(jax.ShapeDtypeStruct((span, cols), bf16...  95.7 us

commit v1 on v0

--- a/solution.py
+++ b/solution.py
@@ -101,11 +101,6 @@
     own_x.start()
     for copy in w_copies:
         copy.start()
-    for step in range(1, max(CHUNKS, pairs)):
-        if step < CHUNKS:
-            send_mem(step)
-        if step < pairs:
-            send_x(step)
 
     z_copies = []
     z_local = []
@@ -172,11 +167,17 @@
             mean = jnp.dot(averager, qkv[i + 1, out_rows, :], preferred_element_type=jnp.float32)
             pooled[i, small_rows, :] = mean.astype(jnp.bfloat16)
 
-    for step in range(max(CHUNKS, pairs)):
+    for step in range(max(CHUNKS, pairs + 1)):
         if step < CHUNKS:
             fetch(step)
-        if step < pairs:
-            project(step)
+        if step + 1 < CHUNKS:
+            send_mem(step + 1)
+        if 1 <= step < pairs:
+            send_x(step)
+        if step == 0:
+            project(0)
+        elif 1 <= step - 1 < pairs:
+            project(step - 1)
 
     for copy in sends + forwards:
         copy.wait_send()
@@ -196,7 +197,8 @@
     half = got.shape[0] // 2
     greet(groups, width, g, c)
     z_copies = []
-    for ch in range(CHUNKS):
+
+    def send_write(ch):
         for o in list(range(1, groups)) + [0]:
             to = lax.rem(g + o, groups)
             piece = pooled[ch // HALVES, wsel[to], ch % HALVES]
@@ -222,6 +224,8 @@
         for at, copy in z_copies:
             if at == ch:
                 copy.wait_recv()
+        if ch + 2 < CHUNKS:
+            send_write(ch + 2)
         for o in list(range(1, width)) + [0]:
             to = lax.rem(c + o, width)
             rbuf[ch, to] = arrived[ch][rsel[to]]
@@ -278,6 +282,8 @@
 
         lax.fori_loop(0, span // block, one, 0)
 
+    send_write(0)
+    send_write(1)
     for step in range(max(heads, CHUNKS)):
         if step < heads:
             attend(step)

time: 228 us -> 219 us (0.961)
  Pallas kernels: 214 us -> 204 us
    pallas_call x1, Pallas kernels: 95.7 us -> 84.8 us  [local(): pl.pallas_call(kernel, out_shape=(jax.ShapeDtypeStruct((span, cols), bf16...]
where the time goes in v1:
time: 219 us; the launch traced here: 217 us
  Pallas kernels  204 us (93%)
  other arithmetic  9.86 us (5%)
  local copies, waits for them, and re-layouts  2.59 us (1%)
    pallas_call x1, Pallas kernels, local(): pl.pallas_call(functools.partial(project_kernel, groups, width, pool), ou...  119 us
    pallas_call x1, Pallas kernels, local(): pl.pallas_call(kernel, out_shape=(jax.ShapeDtypeStruct((span, cols), bf16...  84.8 us

profile of v1, /device:TPU:11, one launch (start us, length us, event | category | flops | bytes accessed | tf_op | source)
XLA Modules:
  0.0 217.2 jit_solution(4836681510860580585)
XLA Ops:
  0.6 0.0 copy-start
  0.7 1.3 compare_reduce_fusion.1
  2.0 0.9 fusion.4
  2.8 0.6 fusion.3.wsel
  3.4 0.8 compare_reduce_fusion
  4.2 0.5 select_reduce_fusion.1.rsel
  4.7 0.7 compare_select_fusion
  5.4 0.1 reshape.79
  5.5 0.0 copy-done
  5.5 0.7 gather_fusion
  6.2 0.1 reshape.78
  6.3 0.7 fusion.5
  7.0 0.2 reduce_window_sum.11
  7.2 0.7 add_select_fusion
  7.9 0.1 select_reduce_fusion
  8.0 0.1 copy.12
  8.1 0.6 reshape.72.pick
  8.8 119.3 %project_and_fetch.1 = (bf16[3,1024,512]{2,1,0:T(8,128)(2,1)}, bf16[2,512,512]{2,1,0:T(8,128)(2,1)}, bf16[4,4,2,128,512]{4,3,2,1,0:T(8,128)(2,1)}) custom-call(s32[8]{0:T(128)} %reshape.72.pick, bf16[128,5120]{1,0:T(8,128)(2,1)} %bitcast.9, bf16[5120,512]{1,0:T(8,128)(2,1)} %wq.1, bf16[5120,512]{1,0:T(8,128)(2,1)} %wk.1, bf16[5120,512]{1,0:T(8,128)(2,1)} %wv.1, ...), custom_call_target="tpu_custom_call" | custom-call | tf_op jit(solution)/shard_map/project_and_fetch/pallas_call | solution.py:324
  128.0 0.0 copy-start.1
  128.0 84.8 %attend_and_write.1 = (bf16[1024,512]{1,0:T(8,128)(2,1)}, bf16[512,4096]{1,0:T(8,128)(2,1)}) custom-call(s32[4]{0:T(128)} %fusion.3.wsel, s32[8]{0:T(128)} %select_reduce_fusion.1.rsel, bf16[3,1024,512]{2,1,0:T(8,128)(2,1)} %get-tuple-element.7.rest_0_, bf16[4096,512]{1,0:T(8,128)(2,1)} %bitcast.7, bf16[2,2,2,128,512]{4,3,2,1,0:T(8,128)(2,1)} %bitcast.10), custom_call_target="tpu_custom_call" | custom-call | tf_op jit(solution)/shard_map/attend_and_write/pallas_call | solution.py:379
  212.8 0.0 copy-done.1
  212.8 0.0 copy-start.2
  212.8 3.4 %broadcast_select_fusion = bf16[1,2,256,4096]{3,2,1,0:T(8,128)(2,1)} fusion(bf16[1,2,256,4096]{3,2,1,0:T(8,128)(2,1)} %bitcast.8, bf16[1,2,256,4096]{3,2,1,0:T(8,128)(2,1)S(1)} %copy-done.1, pred[]{:T(512)} %compare_reduce_fusion.1), kind=kLoop, calls=%fused_computation.1 | loop fusion | flops 2097152 | bytes 12582913 | tf_op jit(solution)/shard_map/jit(_where)/select_n | solution.py:408
  216.2 1.0 copy.14
  (3 shorter events, 0.0 us)
Async XLA Ops:
  0.6 4.9 %copy-start = (s32[32]{0:T(128)S(1)}, s32[32]{0:T(128)}, u32[]{:S(2)}) copy-start(s32[32]{0:T(128)} %param.14) | copy-start | bytes 388
  128.0 84.8 %copy-start.1 = (bf16[1,2,256,4096]{3,2,1,0:T(8,128)(2,1)S(1)}, bf16[1,2,256,4096]{3,2,1,0:T(8,128)(2,1)}, u32[]{:S(2)}) copy-start(bf16[1,2,256,4096]{3,2,1,0:T(8,128)(2,1)} %param.12) | copy-start | bytes 12582916
  212.8 3.4 %copy-start.2 = (bf16[1024,512]{1,0:T(8,128)(2,1)S(1)}, bf16[1024,512]{1,0:T(8,128)(2,1)}, u32[]{:S(2)}) copy-start(bf16[1024,512]{1,0:T(8,128)(2,1)} %get-tuple-element.10) | copy-start | bytes 3145732

commit v2 on v1

--- a/solution.py
+++ b/solution.py
@@ -34,7 +34,7 @@
     pl.semaphore_wait(barrier, width + groups - 2)
 
 
-def project_kernel(groups, width, pool, pick, x, wq, wk, wv, mem, qkv, pooled, got, *scratch):
+def project_kernel(groups, width, pool, selected, frame_slot, x, wq, wk, wv, mem, qkv, pooled, got, *scratch):
     rows = scratch[:CHUNKS]
     (sendbuf, xg, w3, w_sem, own_sem, mem_send, mem_recv, x_send, x_recv, f_send, f_recv,
      z_send, z_recv, z_own) = scratch[CHUNKS:]
@@ -105,6 +105,19 @@
     z_copies = []
     z_local = []
 
+    def picks_of(to):
+        found = [jnp.int32(0)] * CAP
+        count = jnp.int32(0)
+        for j in range(SEL):
+            slot = frame_slot[selected[to, j]]
+            here = lax.div(slot, width) == g
+            column = lax.rem(slot, width)
+            found = [jnp.where(here & (count == r), column, found[r]) for r in range(CAP)]
+            count = count + jnp.where(here, 1, 0)
+        return found
+
+    picks = [picks_of(lax.rem(g + o, groups)) for o in range(groups)]
+
     def fetch(ch):
         own[ch].wait()
         for o in range(1, width):
@@ -112,7 +125,7 @@
         for o in list(range(1, groups)) + [0]:
             to = lax.rem(g + o, groups)
             for r in range(CAP):
-                sendbuf[ch, to, r] = rows[ch][pick[to * CAP + r]]
+                sendbuf[ch, to, r] = rows[ch][picks[o][r]]
             if o == 0:
                 copy = pltpu.make_async_copy(sendbuf.at[ch, g], got.at[ch, g], z_own.at[ch])
                 z_local.append(copy)
@@ -187,7 +200,7 @@
         copy.wait()
 
 
-def attend_kernel(groups, width, wsel, rsel, bias, qkv, got, pooled, att, assembled, *scratch):
+def attend_kernel(groups, width, write_slot, bias, qkv, got, pooled, att, assembled, *scratch):
     arrived = scratch[:CHUNKS]
     wbuf, rbuf, z_send, z_recv, r_send, r_recv, r_own = scratch[CHUNKS:]
     g = lax.axis_index("mem")
@@ -198,10 +211,26 @@
     greet(groups, width, g, c)
     z_copies = []
 
+    def frame_for(to):
+        found = jnp.int32(0)
+        for f in range(FRAMES_SPAN):
+            found = jnp.where(lax.div(write_slot[g, f], width) == to, f, found)
+        return found
+
+    def span_for(to):
+        found = jnp.int32(0)
+        for span_id in range(groups):
+            for f in range(FRAMES_SPAN):
+                found = jnp.where(write_slot[span_id, f] == g * width + to, span_id, found)
+        return found
+
+    wsel = [frame_for(lax.rem(g + o, groups)) for o in range(groups)]
+    rsel = [span_for(lax.rem(c + o, width)) for o in range(width)]
+
     def send_write(ch):
         for o in list(range(1, groups)) + [0]:
             to = lax.rem(g + o, groups)
-            piece = pooled[ch // HALVES, wsel[to], ch % HALVES]
+            piece = pooled[ch // HALVES, wsel[o], ch % HALVES]
             if o == 0:
                 arrived[ch][g] = piece
                 continue
@@ -228,7 +257,7 @@
             send_write(ch + 2)
         for o in list(range(1, width)) + [0]:
             to = lax.rem(c + o, width)
-            rbuf[ch, to] = arrived[ch][rsel[to]]
+            rbuf[ch, to] = arrived[ch][rsel[o]]
             place = assembled.at[
                 pl.ds(ch * TOK, TOK), pl.ds(pl.multiple_of(c * cols, cols), cols)
             ]
@@ -309,13 +338,6 @@
     pool = span // (FRAMES_SPAN * MTOK)
     features = memory_kv.shape[3]
 
-    slot_ids = jnp.take(frame_slot, selected, axis=0)
-    slot_row = slot_ids // width
-    in_row = slot_row == g
-    rank = jnp.cumsum(in_row.astype(jnp.int32), axis=1) - 1
-    hit = in_row[:, None, :] & (rank[:, None, :] == jnp.arange(CAP, dtype=jnp.int32)[None, :, None])
-    pick = jnp.sum(jnp.where(hit, (slot_ids % width)[:, None, :], 0), axis=2).reshape(-1)
-
     vmem = pl.BlockSpec(memory_space=pltpu.VMEM)
     smem = pl.BlockSpec(memory_space=pltpu.SMEM)
     anywhere = pl.BlockSpec(memory_space=pl.ANY)
@@ -328,7 +350,7 @@
             jax.ShapeDtypeStruct((2, FRAMES_SPAN * MTOK, cols), bf16),
             jax.ShapeDtypeStruct((CHUNKS, groups, CAP, TOK, cols), bf16),
         ),
-        in_specs=[smem] + [anywhere] * 5,
+        in_specs=[smem] * 2 + [anywhere] * 5,
         out_specs=(vmem, vmem, anywhere),
         scratch_shapes=[pltpu.VMEM((width, TOK, cols), bf16)] * CHUNKS
         + [
@@ -351,23 +373,23 @@
             collective_id=0, has_side_effects=True, vmem_limit_bytes=VMEM_LIMIT
         ),
         name="project_and_fetch",
-    )(pick, span_input[0], w_query, w_key, w_value, memory_kv.reshape(2 * MTOK, features))
-
-    own_slots = lax.dynamic_index_in_dim(write_slot, g, 0, keepdims=False)
-    rows_m = jnp.arange(groups, dtype=jnp.int32)
-    frames = jnp.arange(FRAMES_SPAN, dtype=jnp.int32)
-    wsel = jnp.sum(
-        jnp.where((own_slots // width)[None, :] == rows_m[:, None], frames[None, :], 0), axis=1
+    )(
+        selected,
+        frame_slot,
+        span_input[0],
+        w_query,
+        w_key,
+        w_value,
+        memory_kv.reshape(2 * MTOK, features),
     )
-    targets = g * width + jnp.arange(width, dtype=jnp.int32)
-    match = jnp.any(write_slot[None, :, :] == targets[:, None, None], axis=2)
-    rsel = jnp.sum(jnp.where(match, rows_m[None, :], 0), axis=1)
-
-    operands = [wsel, rsel]
-    specs = [smem, smem]
+
+    operands = [write_slot]
+    specs = [smem]
     kernel = functools.partial(attend_kernel, groups, width)
     if groups * CAP != SEL:
-        own_rows = lax.dynamic_index_in_dim(slot_row, g, 0, keepdims=False)
+        own_ids = lax.dynamic_index_in_dim(selected, g, 0, keepdims=False)
+        own_rows = jnp.take(frame_slot, own_ids, axis=0) // width
+        rows_m = jnp.arange(groups, dtype=jnp.int32)
         counts = jnp.sum((own_rows[None, :] == rows_m[:, None]).astype(jnp.int32), axis=1)
         live = jnp.arange(CAP, dtype=jnp.int32)[None, :] < counts[:, None]
         fill = jnp.where(live, 0.0, NEG_FILL).astype(jnp.float32)
@@ -409,8 +431,8 @@
     return (attended[None], new_memory)
 
 
-def without_bias(kernel, wsel, rsel, *rest):
-    kernel(wsel, rsel, None, *rest)
+def without_bias(kernel, write_slot, *rest):
+    kernel(write_slot, None, *rest)
 
 
 def solution(mesh):

time: 219 us -> 212 us (0.968)
  other arithmetic: 9.86 us -> 6.01 us
    select_n x3 -> x0, other arithmetic: 2.24 us -> none  [the longest x1 0.87 us: local(): own_slots // width]
where the time goes in v2:
time: 212 us
  Pallas kernels  204 us (96%)
  other arithmetic  6.01 us (3%)
    pallas_call x1, Pallas kernels, local(): pl.pallas_call(functools.partial(project_kernel, groups, width, pool), ou...  119 us
    pallas_call x1, Pallas kernels, local(): pl.pallas_call(kernel, out_shape=(jax.ShapeDtypeStruct((span, cols), bf16...  84.6 us
    select_n x1, other arithmetic, local(): jnp.where(written, assembled.reshape(memory_kv.shape), memory_kv)  5.38 us

profile of v2, /device:TPU:11, one launch (start us, length us, event | category | flops | bytes accessed | tf_op | source)
XLA Modules:
  0.0 212.2 jit_solution(5039427376776747222)
XLA Ops:
  0.6 0.0 copy-start.1
  0.6 119.3 %project_and_fetch.1 = (bf16[3,1024,512]{2,1,0:T(8,128)(2,1)}, bf16[2,512,512]{2,1,0:T(8,128)(2,1)}, bf16[4,4,2,128,512]{4,3,2,1,0:T(8,128)(2,1)}) custom-call(s32[4,8]{1,0:T(4,128)} %selected.1, s32[32]{0:T(128)} %frame_slot.1, bf16[128,5120]{1,0:T(8,128)(2,1)} %bitcast.9, bf16[5120,512]{1,0:T(8,128)(2,1)} %wq.1, bf16[5120,512]{1,0:T(8,128)(2,1)} %wk.1, ...), custom_call_target="tpu_custom_call" | custom-call | tf_op jit(solution)/shard_map/project_and_fetch/pallas_call | solution.py:346
  119.9 0.0 copy-done.1
  119.9 0.7 copy.10.write_slot
  120.6 84.6 %attend_and_write.1 = (bf16[1024,512]{1,0:T(8,128)(2,1)}, bf16[512,4096]{1,0:T(8,128)(2,1)}) custom-call(s32[4,2]{1,0:T(4,128)} %copy.10.write_slot, bf16[3,1024,512]{2,1,0:T(8,128)(2,1)} %get-tuple-element.7.rest_0_, bf16[4096,512]{1,0:T(8,128)(2,1)} %bitcast.7, bf16[2,2,2,128,512]{4,3,2,1,0:T(8,128)(2,1)} %bitcast.10), custom_call_target="tpu_custom_call" | custom-call | tf_op jit(solution)/shard_map/attend_and_write/pallas_call | solution.py:401
  205.2 0.6 compare_reduce_fusion
  205.8 0.0 copy-start
  205.8 5.4 %broadcast_select_fusion = bf16[1,2,256,4096]{3,2,1,0:T(8,128)(2,1)} fusion(bf16[1,2,256,4096]{3,2,1,0:T(8,128)(2,1)} %bitcast.8, bf16[1,2,256,4096]{3,2,1,0:T(8,128)(2,1)} %param.12, pred[]{:T(512)} %compare_reduce_fusion), kind=kLoop, calls=%fused_computation | loop fusion | flops 2097152 | bytes 12582913 | tf_op jit(solution)/shard_map/jit(_where)/select_n | solution.py:430
  211.2 0.0 copy-done
  211.2 1.0 copy.12
Async XLA Ops:
  0.6 119.3 %copy-start.1 = (s32[4,2]{0,1:T(2,128)S(1)}, s32[4,2]{0,1:T(2,128)}, u32[]{:S(2)}) copy-start(s32[4,2]{0,1:T(2,128)} %param.15) | copy-start | bytes 100
  205.8 5.4 %copy-start = (bf16[1024,512]{1,0:T(8,128)(2,1)S(1)}, bf16[1024,512]{1,0:T(8,128)(2,1)}, u32[]{:S(2)}) copy-start(bf16[1024,512]{1,0:T(8,128)(2,1)} %get-tuple-element.10) | copy-start | bytes 3145732
